TPU v7x, 256 devices: a whole 4x4x8 slice. The times are simulated.
256 devices in a mesh: seq: 32 (over z, y), head: 8 (over x, core).
Axes of the slice: x: 4, y: 4, z: 8, core: 2. Of those that a mesh axis runs over, the one named last changes fastest.
Arguments:
- grad_y: bfloat16 [16384, 4096], P('seq', 'head'), may hold values from -6 to 6
- w_out: bfloat16 [4096, 4096], P('head'), may hold values from -0.09375 to 0.09375
- queries: bfloat16 [16384, 4096], P('seq', 'head'), may hold values from -6 to 6
- keys: bfloat16 [16384, 4096], P('seq', 'head'), may hold values from -6 to 6
- values: bfloat16 [16384, 4096], P('seq', 'head'), may hold values from -6 to 6
- level_rows: int32 [16384], P('seq'), may hold values from 0 to 127
- level_table: float32 [128, 12, 32], P(None, None, 'head'), may hold values from 0.2 to 3
Outputs:
- query_grad: float32 [16384, 4096], P('seq', 'head')
- key_grad: float32 [16384, 4096], P('seq', 'head')
- value_grad: float32 [16384, 4096], P('seq', 'head')
Inputs may be any that keep to these rules, and one draw needn't show every extreme that they name: `level_rows`: each token names one row of the level-weight table.
All inputs are finite; a program needn't handle non-finite values.
Results may differ from a plain program's by a relative error of at most 0.0049.
Values may be sent and summed in bfloat16 or wider, within the bound.
A program may use at most 128 MiB of HBM per device.

v0:
```python
import jax
import jax.numpy as jnp
from jax import lax
from jax.sharding import PartitionSpec as P

BLK = 128


def level_norm(level_count, block_size, head_size):
    level_ids = jnp.arange(level_count, dtype=jnp.int32)
    doubling = jnp.exp2(jnp.maximum(level_ids - 1, 0).astype(jnp.float32))
    return lax.rsqrt(doubling * float(block_size * head_size))


def sibling(states, bit_index):
    block_count = states.shape[0]
    span = 2**bit_index
    grouped = states.reshape((block_count // span, span) + states.shape[1:]).sum(axis=1)
    paired = grouped.reshape((block_count // (2 * span), 2) + grouped.shape[1:])[:, ::-1]
    return jnp.repeat(paired.reshape(grouped.shape), span, axis=0)


def shards(grad_y, w_out, queries, keys, values, level_rows, level_table):
    token_count, width = queries.shape
    table_size, level_count, head_count = level_table.shape
    head_size = width // head_count
    block_count = token_count // BLK
    local_bits = block_count.bit_length() - 1
    device_bits = lax.axis_size("seq").bit_length() - 1
    position = lax.axis_index("seq")
    highest = lax.Precision.HIGHEST
    columns = w_out
    grad_sum = lax.dot_general(
        lax.all_gather(grad_y, "head", axis=1, tiled=True),
        columns,
        (((1,), (1,)), ((), ())),
        preferred_element_type=jnp.float32,
    )
    grad_out = grad_sum.astype(jnp.bfloat16)
    one_hot = (level_rows[:, None] == jnp.arange(table_size, dtype=jnp.int32)[None, :]).astype(
        jnp.float32
    )
    weights = jnp.dot(
        one_hot, level_table.reshape(table_size, level_count * head_count), precision=highest
    )
    weights = (
        weights.reshape(token_count, level_count, head_count)
        * level_norm(level_count, BLK, head_size)[None, :, None]
    )
    block_shape = (block_count, BLK, head_count, head_size)
    query_blocks = queries.reshape(block_shape)
    key_blocks = keys.reshape(block_shape)
    value_blocks = values.reshape(block_shape)
    grad_blocks = grad_out.reshape(block_shape)
    weight_blocks = weights.reshape(block_count, BLK, level_count, head_count)
    causal = (jnp.arange(BLK)[:, None] >= jnp.arange(BLK)[None, :]).astype(jnp.float32)
    intra_weight = jnp.transpose(weight_blocks[:, :, 0, :], (0, 2, 1))[:, :, :, None] * causal
    intra_grad = (
        jnp.einsum("bthp,bshp->bhts", grad_blocks, value_blocks, preferred_element_type=jnp.float32)
        * intra_weight
    ).astype(jnp.bfloat16)
    intra_score = (
        jnp.einsum("bthp,bshp->bhts", query_blocks, key_blocks, preferred_element_type=jnp.float32)
        * intra_weight
    ).astype(jnp.bfloat16)
    query_grad = jnp.einsum(
        "bhts,bshp->bthp", intra_grad, key_blocks, preferred_element_type=jnp.float32
    )
    key_grad = jnp.einsum(
        "bhts,bthp->bshp", intra_grad, query_blocks, preferred_element_type=jnp.float32
    )
    value_grad = jnp.einsum(
        "bhts,bthp->bshp", intra_score, grad_blocks, preferred_element_type=jnp.float32
    )
    states = jnp.einsum(
        "bthi,bthj->bhij", key_blocks, value_blocks, preferred_element_type=jnp.float32
    )
    block_ids = jnp.arange(block_count, dtype=jnp.int32)
    adjoint = jnp.zeros_like(states)
    for bit_index in range(local_bits):
        present = (block_ids >> bit_index & 1).astype(jnp.float32)[:, None, None, None]
        bucket = (sibling(states, bit_index) * present).astype(jnp.bfloat16)
        level_weight = weight_blocks[:, :, bit_index + 1, :][..., None]
        query_grad = query_grad + level_weight * jnp.einsum(
            "bthj,bhij->bthi", grad_blocks, bucket, preferred_element_type=jnp.float32
        )
        weighted = (level_weight * query_blocks).astype(jnp.bfloat16)
        adjoint_part = (
            jnp.einsum("bthi,bthj->bhij", weighted, grad_blocks, preferred_element_type=jnp.float32)
            * present
        )
        adjoint = adjoint + sibling(adjoint_part, bit_index)
    flat_query = queries.reshape(token_count, head_count, head_size)
    flat_grad = grad_out.reshape(token_count, head_count, head_size)
    device_total = states.sum(axis=0)
    device_flags = [
        (position >> bit_index & 1).astype(jnp.float32) for bit_index in range(device_bits)
    ]
    device_parts = []
    for bit_index in range(device_bits):
        level_weight = weights[:, local_bits + bit_index + 1, :][..., None]
        weighted = (level_weight * flat_query).astype(jnp.bfloat16)
        device_parts.append(
            jnp.einsum("thi,thj->hij", weighted, flat_grad, preferred_element_type=jnp.float32)
            * device_flags[bit_index]
        )

    def membership(row_count):
        peers = jnp.arange(row_count, dtype=jnp.int32)
        columns = []
        for bit_index in range(device_bits):
            inside = (
                (peers >> bit_index + 1 == position >> bit_index + 1)
                & (peers >> bit_index & 1 == 0)
                & (position >> bit_index & 1 == 1)
            )
            columns.append(inside.astype(jnp.float32))
        return jnp.stack(columns, axis=1)

    segment = lax.all_gather(device_total[None], "seq", axis=0, tiled=True)
    stacked = jnp.einsum("ne,nhij->ehij", membership(segment.shape[0]), segment, precision=highest)
    buckets = [stacked[bit_index] for bit_index in range(device_bits)]
    adjoint_stack = jnp.stack(device_parts, axis=0)
    carried = lax.psum_scatter(
        jnp.einsum(
            "ne,ehij->nhij", membership(lax.axis_size("seq") * 1), adjoint_stack, precision=highest
        ),
        "seq",
        scatter_dimension=0,
        tiled=True,
    )[0]
    for bit_index in range(device_bits):
        level_weight = weight_blocks[:, :, local_bits + bit_index + 1, :][..., None]
        query_grad = query_grad + level_weight * jnp.einsum(
            "bthj,hij->bthi",
            grad_blocks,
            buckets[bit_index].astype(jnp.bfloat16),
            preferred_element_type=jnp.float32,
        )
    adjoint_all = (adjoint + carried[None]).astype(jnp.bfloat16)
    key_grad = key_grad + jnp.einsum(
        "bshj,bhij->bshi", value_blocks, adjoint_all, preferred_element_type=jnp.float32
    )
    value_grad = value_grad + jnp.einsum(
        "bshi,bhij->bshj", key_blocks, adjoint_all, preferred_element_type=jnp.float32
    )
    return (
        query_grad.reshape(token_count, width),
        key_grad.reshape(token_count, width),
        value_grad.reshape(token_count, width),
    )


def solution(mesh):
    return jax.shard_map(
        shards,
        mesh=mesh,
        in_specs=(
            P("seq", "head"),
            P("head", None),
            P("seq", "head"),
            P("seq", "head"),
            P("seq", "head"),
            P("seq"),
            P(None, None, "head"),
        ),
        out_specs=(P("seq", "head"), P("seq", "head"), P("seq", "head")),
        check_vma=False,
    )
```

profile of v0, /device:TPU:2, one launch (start us, length us, event | category | flops | bytes accessed | tf_op | source)
XLA Modules:
  0.0 390.7 jit_solution(12083027111815541625)
XLA Ops:
  8.0 1.2 reshape.258
  9.1 1.4 reshape.261
  10.5 1.1 bitcast_reduce_fusion.1
  13.0 1.3 copy.198
  14.4 32.1 %all-gather.4.cloned.1.call-done = bf16[512,4096]{1,0:T(8,128)(2,1)} async-done(((bf16[512,512]{1,0:T(8,128)(2,1)}), bf16[512,4096]{1,0:T(8,128)(2,1)}) %all-gather.4.cloned.1.call-update) | async-done | bytes 4194320 | tf_op jit(solution)/shard_map/all_gather | solution.py:34
  46.5 5.8 %convolution_convert_fusion = bf16[512,512]{0,1:T(8,128)(2,1)S(1)} fusion(bf16[512,4096]{1,0:T(8,128)(2,1)} %all-gather.4.cloned.1.call-done, bf16[512,4096]{1,0:T(8,128)(2,1)} %param.8), kind=kOutput, calls=%fused_computation.40 | convolution fusion | flops 2147745792 | bytes 8912896 | tf_op jit(solution)/shard_map/dot_general | solution.py:33
  53.9 3.9 %fusion.2 = f32[32,4,128,128]{3,0,2,1:T(8,128)S(1)} fusion(f32[5,4,128,128]{3,2,1,0:T(8,128)S(1)} %fusion.27, pred[32,5]{0,1:T(8,128)(4,1)S(1)} %stack.17), kind=kOutput, calls=%fused_computation.2 | convolution fusion | flops 125829120 | bytes 9699488 | tf_op jit(solution)/shard_map/ne,ehij->nhij/dot_general | solution.py:125
  57.8 8.3 %copy.168 = f32[32,4,128,128]{3,2,1,0:T(8,128)} copy(f32[32,4,128,128]{3,0,2,1:T(8,128)S(1)} %fusion.2) | data formatting | bytes 16777216 | tf_op jit(solution)/shard_map/ne,ehij->nhij/dot_general | solution.py:125
  67.3 1.1 rev.8
  69.3 2.0 fusion.39
  73.5 1.1 reverse_add_fusion
  74.6 2.5 copy.156
  77.7 1.3 convolution_bitcast_fusion.1
  79.1 1.3 convolution_bitcast_fusion.9
  80.3 1.7 fusion.25
  82.0 1.9 fusion.22
  83.9 1.6 fusion.20
  85.4 63.2 %all-gather.6.cloned.1.call-done = f32[128,128,128]{2,1,0:T(8,128)} async-done(((f32[4,128,128]{2,1,0:T(8,128)}), f32[128,128,128]{2,1,0:T(8,128)}) %all-gather.6.cloned.1.call-update) | async-done | bytes 8388624 | tf_op jit(solution)/shard_map/all_gather | solution.py:120
  148.6 10.5 %fusion.4 = bf16[5,4,128,128]{3,0,2,1:T(8,128)(2,1)S(1)} fusion(f32[32,4,128,128]{3,2,1,0:T(8,128)} %bitcast.212, pred[32,5]{0,1:T(8,128)(4,1)S(1)} %stack.17), kind=kOutput, calls=%fused_computation.6 | convolution fusion | flops 126156800 | bytes 9044128 | tf_op jit(solution)/shard_map/ne,nhij->ehij/dot_general | solution.py:121
  164.3 1.0 copy.312
  165.4 213.6 %reduce-scatter.2.cloned.1.call-done = f32[1,4,128,128]{3,2,1,0:T(8,128)} async-done(((f32[32,4,128,128]{3,2,1,0:T(8,128)}), f32[1,4,128,128]{3,2,1,0:T(8,128)}) %reduce-scatter.2.cloned.1.call-update) | async-done | bytes 262160 | tf_op jit(solution)/shard_map/reduce_scatter | solution.py:124
  378.9 1.1 copy.169
  381.2 1.0 copy.311
  383.1 1.0 copy.310
  (81 shorter events, 15.6 us)
Async XLA Ops:
  7.2 5.4 %copy-start = (f32[128,12,4]{0,2,1:T(4,128)S(1)}, f32[128,12,4]{0,2,1:T(4,128)}, u32[]{:S(2)}) copy-start(f32[128,12,4]{0,2,1:T(4,128)} %param.13) | copy-start | bytes 73732
  7.2 39.3 %all-gather.4.cloned.1.call-start = ((), (), s32[]{:S(2)}) async-start(), calls=%async_computation.1 | async-start | bytes 4718592 | tf_op jit(solution)/shard_map/all_gather | solution.py:34
  7.9 140.7 %all-gather.6.cloned.1.call-start = ((), (), s32[]{:S(2)}) async-start(), calls=%async_computation.3 | async-start | bytes 8650752 | tf_op jit(solution)/shard_map/all_gather | solution.py:120
  9.1 3.3 copy-start.2
  10.5 2.1 copy-start.12
  12.5 366.5 %reduce-scatter.2.cloned.1.call-start = ((), (), s32[]{:S(2)}) async-start(), calls=%async_computation.2 | async-start | bytes 8650752 | tf_op jit(solution)/shard_map/reduce_scatter | solution.py:124
  66.1 1.0 copy-start.8
  67.3 1.1 copy-start.9
  68.4 2.9 copy-start.7
  73.5 3.6 copy-start.3
  82.0 1.9 copy-start.10
  159.1 1.2 copy-start.5
  163.6 216.4 %copy-start.6 = (f32[2,2,4,128,128]{3,4,2,1,0:T(8,128)S(1)}, f32[2,2,4,128,128]{3,4,2,1,0:T(8,128)}, u32[]{:S(2)}) copy-start(f32[2,2,4,128,128]{3,4,2,1,0:T(8,128)} %copy.156) | copy-start | bytes 3145732
  164.3 215.8 %copy-start.4 = (f32[4,128,4,128]{3,1,2,0:T(8,128)S(1)}, f32[4,128,4,128]{3,1,2,0:T(8,128)}, u32[]{:S(2)}) copy-start(f32[4,128,4,128]{3,1,2,0:T(8,128)} %convolution_bitcast_fusion.1) | copy-start | bytes 3145732
  380.5 1.7 copy-start.11
  382.2 1.9 copy-start.1
Sparse Core Ops, SparseCore 0:
  9.9 36.5 all-gather.3
  49.1 99.5 all-gather.5
  152.7 226.2 reduce-scatter.1
where the time goes:
time: 391 us
  waiting for transfers between devices  310 us (79%)
  matrix products  37.4 us (10%)
  local copies, waits for them, and re-layouts  25.1 us (6%)
  between operations  14.2 us (4%)
  other arithmetic  4.28 us (1%)
    reduce_scatter x1, waiting for transfers between devices, shards(): lax.psum_scatter(jnp.einsum('ne,ehij->nhij', membership(lax.axis_size('se...  214 us
    all_gather x1, waiting for transfers between devices, shards(): segment = lax.all_gather(device_total[None], 'seq', axis=0, tiled=True)  63.2 us
    all_gather x1, waiting for transfers between devices, shards(): lax.all_gather(grad_y, 'head', axis=1, tiled=True)  32.1 us
    dot_general x1, matrix products, shards(): jnp.einsum('ne,nhij->ehij', membership(segment.shape[0]), segment, precis...  10.5 us
    dot_general x1, local copies, waits for them, and re-layouts, shards(): jnp.einsum('ne,ehij->nhij', membership(lax.axis_size('seq') * 1), adjoint...  8.28 us
  transfers between devices with their start and end apart: 3, of which 3 were waited for; matrix products, arithmetic and copies ran while one was open for 15% of the time, Pallas kernels for 0%

commit v1 on v0

--- a/solution.py
+++ b/solution.py
@@ -4,6 +4,27 @@
 from jax.sharding import PartitionSpec as P
 
 BLK = 128
+
+
+def collect(value, axis, dim):
+    size, index, rows = (lax.axis_size(axis), lax.axis_index(axis), value.shape[dim])
+    right = [(i, (i + 1) % size) for i in range(size)]
+    left = [(i, (i - 1) % size) for i in range(size)]
+    out = jnp.zeros((*value.shape[:dim], size * rows, *value.shape[dim + 1 :]), value.dtype)
+    out = lax.dynamic_update_slice_in_dim(out, value, index * rows, axis=dim)
+    from_left = from_right = value
+    middle = size // 2
+    for step in range(1, middle + 1):
+        from_left = lax.ppermute(from_left, axis, right)
+        out = lax.dynamic_update_slice_in_dim(
+            out, from_left, (index - step) % size * rows, axis=dim
+        )
+        if step < size - middle:
+            from_right = lax.ppermute(from_right, axis, left)
+            out = lax.dynamic_update_slice_in_dim(
+                out, from_right, (index + step) % size * rows, axis=dim
+            )
+    return out
 
 
 def level_norm(level_count, block_size, head_size):
@@ -31,7 +52,7 @@
     highest = lax.Precision.HIGHEST
     columns = w_out
     grad_sum = lax.dot_general(
-        lax.all_gather(grad_y, "head", axis=1, tiled=True),
+        collect(grad_y, "head", 1),
         columns,
         (((1,), (1,)), ((), ())),
         preferred_element_type=jnp.float32,

time: 391 us -> 363 us (0.928)
  waiting for transfers between devices: 310 us -> 263 us
  local copies, waits for them, and re-layouts: 25.1 us -> 36 us
  starting transfers between devices: 0.12 us -> 5.45 us
    all_gather x1, waiting for transfers between devices: 63.2 us -> 28.4 us  [shards(): segment = lax.all_gather(device_total[None], 'seq', axis=0, tiled=True)]
    all_gather x1 -> x0, waiting for transfers between devices: 32.1 us -> none  [shards(): lax.all_gather(grad_y, 'head', axis=1, tiled=True)]
    ppermute x0 -> x7, waiting for transfers between devices: none -> 21.2 us  [the longest x4 21.2 us: collect(): from_left = lax.ppermute(from_left, axis, right)]
    dynamic_update_slice x0 -> x8, local copies, waits for them, and re-layouts: none -> 5.89 us  [the longest x4 2.35 us: collect(): lax.dynamic_update_slice_in_dim(out, from_left, (index - step) % size * r...]
    ppermute x0 -> x7, starting transfers between devices: none -> 5.37 us  [the longest x3 5.35 us: collect(): from_right = lax.ppermute(from_right, axis, left)]
  transfers between devices with their start and end apart: 3 -> 9, of which waited for: 3 -> 6; matrix products, arithmetic and copies ran while one was open for 15% -> 17% of each run, Pallas kernels for 0% -> 0%
where the time goes in v1:
time: 363 us; the launch traced here: 362 us
  waiting for transfers between devices  263 us (72%)
  matrix products  37.2 us (10%)
  local copies, waits for them, and re-layouts  36 us (10%)
  between operations  14.8 us (4%)
  other arithmetic  5.74 us (2%)
  starting transfers between devices  5.45 us (2%)
    reduce_scatter x1, waiting for transfers between devices, shards(): lax.psum_scatter(jnp.einsum('ne,ehij->nhij', membership(lax.axis_size('se...  213 us
    all_gather x1, waiting for transfers between devices, shards(): segment = lax.all_gather(device_total[None], 'seq', axis=0, tiled=True)  28.4 us
    ppermute x4, waiting for transfers between devices, collect(): from_left = lax.ppermute(from_left, axis, right)  21.2 us
    dot_general x1, matrix products, shards(): jnp.einsum('ne,nhij->ehij', membership(segment.shape[0]), segment, precis...  10.6 us
    dot_general x1, local copies, waits for them, and re-layouts, shards(): jnp.einsum('ne,ehij->nhij', membership(lax.axis_size('seq') * 1), adjoint...  8.26 us
  transfers between devices with their start and end apart: 9, of which 6 were waited for; matrix products, arithmetic and copies ran while one was open for 17% of the time, Pallas kernels for 0%

profile of v1, /device:TPU:2, one launch (start us, length us, event | category | flops | bytes accessed | tf_op | source)
XLA Modules:
  0.0 362.0 jit_solution(10948709033159824583)
XLA Ops:
  11.7 1.7 collective-permute-start.1
  13.8 6.4 %collective-permute-done = bf16[512,512]{1,0:T(8,128)(2,1)S(1)} collective-permute-done((bf16[512,512]{1,0:T(8,128)(2,1)S(1)}, bf16[512,512]{1,0:T(8,128)(2,1)S(1)}, u32[]{:S(2)}, u32[]{:S(2)}) %collective-permute-start) | collective-permute-done | bytes 524320 | tf_op jit(solution)/shard_map/ppermute | solution.py:18
  20.3 2.0 collective-permute-start.3
  22.3 6.7 %collective-permute-done.2 = bf16[512,512]{1,0:T(8,128)(2,1)} collective-permute-done((bf16[512,512]{1,0:T(8,128)(2,1)S(1)}, bf16[512,512]{1,0:T(8,128)(2,1)}, u32[]{:S(2)}, u32[]{:S(2)}) %collective-permute-start.2) | collective-permute-done | bytes 524320 | tf_op jit(solution)/shard_map/ppermute | solution.py:18
  32.4 1.6 collective-permute-start.5
  34.1 3.8 %collective-permute-done.4 = bf16[512,512]{1,0:T(8,128)(2,1)} collective-permute-done((bf16[512,512]{1,0:T(8,128)(2,1)}, bf16[512,512]{1,0:T(8,128)(2,1)}, u32[]{:S(2)}, u32[]{:S(2)}) %collective-permute-start.4) | collective-permute-done | bytes 524320 | tf_op jit(solution)/shard_map/ppermute | solution.py:18
  42.5 4.3 %collective-permute-done.6 = bf16[512,512]{1,0:T(8,128)(2,1)S(1)} collective-permute-done((bf16[512,512]{1,0:T(8,128)(2,1)}, bf16[512,512]{1,0:T(8,128)(2,1)S(1)}, u32[]{:S(2)}, u32[]{:S(2)}) %collective-permute-start.6) | collective-permute-done | bytes 524320 | tf_op jit(solution)/shard_map/ppermute | solution.py:18
  46.8 2.4 convolution_convert_fusion
  50.8 3.9 %fusion.2 = f32[32,4,128,128]{3,0,2,1:T(8,128)S(1)} fusion(f32[5,4,128,128]{3,2,1,0:T(8,128)S(1)} %fusion.27, pred[32,5]{0,1:T(8,128)(4,1)S(1)} %stack.17), kind=kOutput, calls=%fused_computation.2 | convolution fusion | flops 125829120 | bytes 9699488 | tf_op jit(solution)/shard_map/ne,ehij->nhij/dot_general | solution.py:146
  54.7 8.3 %copy.168 = f32[32,4,128,128]{3,2,1,0:T(8,128)} copy(f32[32,4,128,128]{3,0,2,1:T(8,128)S(1)} %fusion.2) | data formatting | bytes 16777216 | tf_op jit(solution)/shard_map/ne,ehij->nhij/dot_general | solution.py:146
  67.5 1.4 fusion.40
  69.1 1.6 bitcast_reduce_fusion
  73.9 2.6 copy.156
  77.0 1.3 convolution_bitcast_fusion.1
  79.6 1.6 fusion.25
  81.3 1.8 fusion.22
  83.1 1.6 fusion.20
  84.7 28.4 %all-gather.3.cloned.1.call-done = f32[128,128,128]{2,1,0:T(8,128)} async-done(((f32[4,128,128]{2,1,0:T(8,128)}), f32[128,128,128]{2,1,0:T(8,128)}) %all-gather.3.cloned.1.call-update) | async-done | bytes 8388624 | tf_op jit(solution)/shard_map/all_gather | solution.py:141
  113.1 10.6 %fusion.4 = bf16[5,4,128,128]{3,0,2,1:T(8,128)(2,1)S(1)} fusion(f32[32,4,128,128]{3,2,1,0:T(8,128)} %bitcast.212, pred[32,5]{0,1:T(8,128)(4,1)S(1)} %stack.17), kind=kOutput, calls=%fused_computation.6 | convolution fusion | flops 126156800 | bytes 9044128 | tf_op jit(solution)/shard_map/ne,nhij->ehij/dot_general | solution.py:142
  129.9 213.1 %reduce-scatter.2.cloned.1.call-done = f32[1,4,128,128]{3,2,1,0:T(8,128)} async-done(((f32[32,4,128,128]{3,2,1,0:T(8,128)}), f32[1,4,128,128]{3,2,1,0:T(8,128)}) %reduce-scatter.2.cloned.1.call-update) | async-done | bytes 262160 | tf_op jit(solution)/shard_map/reduce_scatter | solution.py:145
  344.1 1.4 fusion.38
  345.6 2.7 fusion.8
  348.3 2.6 copy.178
  350.8 2.3 copy.310
  (101 shorter events, 33.1 us)
Async XLA Ops:
  7.2 6.3 %copy-start = (f32[128,12,4]{0,2,1:T(4,128)S(1)}, f32[128,12,4]{0,2,1:T(4,128)}, u32[]{:S(2)}) copy-start(f32[128,12,4]{0,2,1:T(4,128)} %param.13) | copy-start | bytes 73732
  7.2 4.5 %copy-start.8 = (bf16[512,512]{1,0:T(8,128)(2,1)S(1)}, bf16[512,512]{1,0:T(8,128)(2,1)}, u32[]{:S(2)}) copy-start(bf16[512,512]{1,0:T(8,128)(2,1)} %param.7) | copy-start | bytes 1572868
  7.2 6.2 %copy-start.11 = (s32[512]{0:T(512)S(1)}, s32[512]{0:T(512)}, u32[]{:S(2)}) copy-start(s32[512]{0:T(512)} %param.12) | copy-start | bytes 6148
  7.2 105.9 %all-gather.3.cloned.1.call-start = ((), (), s32[]{:S(2)}) async-start(), calls=%async_computation.2 | async-start | bytes 8650752 | tf_op jit(solution)/shard_map/all_gather | solution.py:141
  9.6 19.5 %copy-start.2 = (bf16[4,128,4,128]{3,2,1,0:T(4,128)(2,1)}, bf16[4,128,4,128]{3,2,1,0:T(4,128)(2,1)S(1)}, u32[]{:S(2)}) copy-start(bf16[4,128,4,128]{3,2,1,0:T(4,128)(2,1)S(1)} %reshape.258) | copy-start | bytes 1572868
  11.6 331.4 %reduce-scatter.2.cloned.1.call-start = ((), (), s32[]{:S(2)}) async-start(), calls=%async_computation.1 | async-start | bytes 8650752 | tf_op jit(solution)/shard_map/reduce_scatter | solution.py:145
  11.7 8.6 %collective-permute-start = (bf16[512,512]{1,0:T(8,128)(2,1)S(1)}, bf16[512,512]{1,0:T(8,128)(2,1)S(1)}, u32[]{:S(2)}, u32[]{:S(2)}) collective-permute-start(bf16[512,512]{1,0:T(8,128)(2,1)S(1)} %copy-done.8), channel_id=1, source_target_pairs={{0,1},{1,2},{2,3},{3,4},{4,5},{5,6},{6,7},{7,0},{8,9},{9,10},{10,1... | collective-permute-start | bytes 1572872 | tf_op jit(solution)/shard_map/ppermute | solution.py:18
  11.7 8.7 %collective-permute-start.1 = (bf16[512,512]{1,0:T(8,128)(2,1)S(1)}, bf16[512,512]{1,0:T(8,128)(2,1)}, u32[]{:S(2)}, u32[]{:S(2)}) collective-permute-start(bf16[512,512]{1,0:T(8,128)(2,1)S(1)} %copy-done.8), channel_id=1, source_target_pairs={{0,7},{1,0},{2,1},{3,2},{4,3},{5,4},{6,5},{7,6},{8,15},{9,8},{10,9... | collective-permute-start | bytes 1572872 | tf_op jit(solution)/shard_map/ppermute | solution.py:23
  20.3 8.9 %copy-start.9 = (bf16[512,512]{1,0:T(8,128)(2,1)}, bf16[512,512]{1,0:T(8,128)(2,1)S(1)}, u32[]{:S(2)}) copy-start(bf16[512,512]{1,0:T(8,128)(2,1)S(1)} %collective-permute-done) | copy-start | bytes 1572868
  20.3 8.7 %collective-permute-start.2 = (bf16[512,512]{1,0:T(8,128)(2,1)S(1)}, bf16[512,512]{1,0:T(8,128)(2,1)}, u32[]{:S(2)}, u32[]{:S(2)}) collective-permute-start(bf16[512,512]{1,0:T(8,128)(2,1)S(1)} %collective-permute-done), channel_id=1, source_target_pairs={{0,1},{1,2},{2,3},{3,4},{4,5},{5,6},{6,7},{7,0},{8,9},{9,10},{10,1... | collective-permute-start | bytes 1572872 | tf_op jit(solution)/shard_map/ppermute | solution.py:18
  20.3 12.0 %collective-permute-start.3 = (bf16[512,512]{1,0:T(8,128)(2,1)}, bf16[512,512]{1,0:T(8,128)(2,1)}, u32[]{:S(2)}, u32[]{:S(2)}) collective-permute-start(bf16[512,512]{1,0:T(8,128)(2,1)} %collective-permute-done.1), channel_id=1, source_target_pairs={{0,7},{1,0},{2,1},{3,2},{4,3},{5,4},{6,5},{7,6},{8,15},{9,8},{10,9... | collective-permute-start | bytes 1572872 | tf_op jit(solution)/shard_map/ppermute | solution.py:23
  29.0 8.9 %collective-permute-start.4 = (bf16[512,512]{1,0:T(8,128)(2,1)}, bf16[512,512]{1,0:T(8,128)(2,1)}, u32[]{:S(2)}, u32[]{:S(2)}) collective-permute-start(bf16[512,512]{1,0:T(8,128)(2,1)} %collective-permute-done.2), channel_id=1, source_target_pairs={{0,1},{1,2},{2,3},{3,4},{4,5},{5,6},{6,7},{7,0},{8,9},{9,10},{10,1... | collective-permute-start | bytes 1572872 | tf_op jit(solution)/shard_map/ppermute | solution.py:18
  29.2 4.9 %copy-start.10 = (bf16[512,512]{1,0:T(8,128)(2,1)S(1)}, bf16[512,512]{1,0:T(8,128)(2,1)}, u32[]{:S(2)}) copy-start(bf16[512,512]{1,0:T(8,128)(2,1)} %copy-done.9) | copy-start | bytes 1572868
  31.1 15.7 %copy-start.12 = (bf16[512,4096]{1,0:T(8,128)(2,1)S(1)}, bf16[512,4096]{1,0:T(8,128)(2,1)}, u32[]{:S(2)}) copy-start(bf16[512,4096]{1,0:T(8,128)(2,1)} %param.8) | copy-start | bytes 12582916
  32.4 10.0 %collective-permute-start.5 = (bf16[512,512]{1,0:T(8,128)(2,1)}, bf16[512,512]{1,0:T(8,128)(2,1)S(1)}, u32[]{:S(2)}, u32[]{:S(2)}) collective-permute-start(bf16[512,512]{1,0:T(8,128)(2,1)} %collective-permute-done.3), channel_id=1, source_target_pairs={{0,7},{1,0},{2,1},{3,2},{4,3},{5,4},{6,5},{7,6},{8,15},{9,8},{10,9... | collective-permute-start | bytes 1572872 | tf_op jit(solution)/shard_map/ppermute | solution.py:23
  37.9 8.8 %collective-permute-start.6 = (bf16[512,512]{1,0:T(8,128)(2,1)}, bf16[512,512]{1,0:T(8,128)(2,1)S(1)}, u32[]{:S(2)}, u32[]{:S(2)}) collective-permute-start(bf16[512,512]{1,0:T(8,128)(2,1)} %collective-permute-done.4), channel_id=1, source_target_pairs={{0,1},{1,2},{2,3},{3,4},{4,5},{5,6},{6,7},{7,0},{8,9},{9,10},{10,1... | collective-permute-start | bytes 1572872 | tf_op jit(solution)/shard_map/ppermute | solution.py:18
  62.9 1.0 copy-start.6
  70.6 5.8 %copy-start.3 = (bf16[4,128,4,128]{3,2,1,0:T(4,128)(2,1)S(1)}, bf16[4,128,4,128]{3,2,1,0:T(4,128)(2,1)}, u32[]{:S(2)}) copy-start(bf16[4,128,4,128]{3,2,1,0:T(4,128)(2,1)} %copy-done.2) | copy-start | bytes 1572868
  78.3 4.7 %copy-start.7 = (bf16[4,4,128,128]{3,2,1,0:T(8,128)(2,1)S(1)}, bf16[4,4,128,128]{3,2,1,0:T(8,128)(2,1)}, u32[]{:S(2)}) copy-start(bf16[4,4,128,128]{3,2,1,0:T(8,128)(2,1)} %fusion.39) | copy-start | bytes 1572868
  113.1 11.5 %copy-start.5 = (f32[4,128,4,128]{3,1,2,0:T(8,128)S(1)}, f32[4,128,4,128]{3,1,2,0:T(8,128)}, u32[]{:S(2)}) copy-start(f32[4,128,4,128]{3,1,2,0:T(8,128)} %fusion.20) | copy-start | bytes 3145732
  344.1 9.0 %copy-start.4 = (f32[4,128,4,128]{3,1,2,0:T(8,128)S(1)}, f32[4,128,4,128]{3,1,2,0:T(8,128)}, u32[]{:S(2)}) copy-start(f32[4,128,4,128]{3,1,2,0:T(8,128)} %convolution_bitcast_fusion.1) | copy-start | bytes 3145732
  350.8 4.3 %copy-start.1 = (f32[128,12,4]{0,2,1:T(4,128)S(1)}, f32[128,12,4]{0,2,1:T(4,128)}, u32[]{:S(2)}) copy-start(f32[128,12,4]{0,2,1:T(4,128)} %param.13) | copy-start | bytes 73732
Sparse Core Ops, SparseCore 0:
  11.7 101.3 all-gather.2
  117.1 225.8 reduce-scatter.1
